TPU v7x, 256 devices: a whole 4x4x8 slice. The times are simulated.
256 devices in a mesh: seq: 64 (over y, z_hi, x), cfg: 2 (over core), clip: 2 (over z_lo).
Axes of the slice: x: 4, y: 4, z: 8 (z_hi: 4, z_lo: 2; z = z_hi * 2 + z_lo), core: 2. Of those that a mesh axis runs over, the one named last changes fastest.
Arguments:
- queries: bfloat16 [2, 2, 2048, 2560], P(None, 'cfg', ('clip', 'seq')), parts along dimension 2, may hold values from -8 to 8
- fresh_kv: bfloat16 [2, 2, 2, 2048, 2560], P(None, 'cfg', None, ('clip', 'seq')), parts along dimension 3, may hold values from -8 to 8
- stale_kv: bfloat16 [2, 2, 2048, 2560], P('cfg', None, ('clip', 'seq')), parts along dimension 2, may hold values from -8 to 8
- timesteps: int32 [2], replicated, may hold values from 0 to 999
- guidance_index: int32 [1], replicated, may hold values from 0 to 11
Outputs:
- guided: bfloat16 [2, 2048, 2560], P(None, ('clip', 'seq'), 'cfg'), parts along dimension 1
There are 2 independent parts, one for each index of `clip`. A program takes and returns all parts, laid end to end along the dimension named above; an argument that names none is the same for every part. Nothing has to cross between parts.
All inputs are finite; a program needn't handle non-finite values.
Results may differ from a plain program's by a relative error of at most 0.0065.
Values may be sent and summed in bfloat16 or wider, within the bound.
A program may use at most 128 MiB of HBM per device.

v0:
```python
import math

import jax
import jax.numpy as jnp
from jax import lax
from jax.sharding import PartitionSpec as P

HEAD_DIM = 128


def partner(shard, axis, distance):
    return lax.ppermute(shard, axis, [(i, i ^ 1 << distance) for i in range(lax.axis_size(axis))])


def gathered_attention(query_rows, key_rows, value_rows):
    count = query_rows.shape[0]
    total = key_rows.shape[0]
    heads = query_rows.shape[1] // HEAD_DIM
    query_heads = query_rows.reshape(count, heads, HEAD_DIM)
    key_heads = key_rows.reshape(total, heads, HEAD_DIM)
    value_heads = value_rows.reshape(total, heads, HEAD_DIM)
    scores = jnp.einsum(
        "qhe,khe->qhk", query_heads, key_heads, preferred_element_type=jnp.float32
    ) / math.sqrt(HEAD_DIM)
    top_score = jnp.max(scores, axis=-1, keepdims=True)
    weights = jnp.exp(scores - top_score)
    totals = jnp.sum(weights, axis=-1)
    summed = jnp.einsum(
        "qhk,khe->qhe",
        weights.astype(jnp.bfloat16),
        value_heads,
        preferred_element_type=jnp.float32,
    )
    return (summed / totals[..., None]).astype(jnp.bfloat16).reshape(count, heads * HEAD_DIM)


def merged_attention(query_rows, own_kv, remote_full, first):
    merged = lax.dynamic_update_slice_in_dim(remote_full, own_kv, first, 1)
    return gathered_attention(query_rows, merged[0], merged[1])


def shards(queries, fresh_kv, stale_kv, timesteps, guidance_index):
    place = lax.axis_index("seq")
    branch = lax.axis_index("cfg")
    tok_rows = queries.shape[2]
    width = queries.shape[3]
    half_width = width // 2
    step_count = queries.shape[0]
    first = place * tok_rows
    previous = jnp.concatenate([stale_kv, fresh_kv[: step_count - 1, 0]], axis=0)
    outputs = []
    for step_no in range(step_count):
        remote_full = lax.all_gather(previous[step_no], "seq", axis=1, tiled=True)
        outputs.append(
            merged_attention(queries[step_no, 0], fresh_kv[step_no, 0], remote_full, first)
        )
    attended = jnp.stack(outputs, axis=0)
    own_start = branch * half_width
    other_start = (1 - branch) * half_width
    mine = lax.dynamic_slice_in_dim(attended, own_start, half_width, 2).astype(jnp.float32)
    outgoing = lax.dynamic_slice_in_dim(attended, other_start, half_width, 2)
    incoming = partner(outgoing, "cfg", 0).astype(jnp.float32)
    is_cond = branch == 0
    cond = jnp.where(is_cond, mine, incoming)
    uncond = jnp.where(is_cond, incoming, mine)
    scale = 1.0 + 0.5 * guidance_index[0].astype(jnp.float32)
    channel_ids = own_start.astype(jnp.float32) + jnp.arange(half_width, dtype=jnp.float32)
    frequency = jnp.exp(-math.log(1000.0) * channel_ids / width)
    gate = 1.0 + 0.5 * jnp.sin(timesteps.astype(jnp.float32)[:, None] * frequency[None, :])
    return (gate[:, None, :] * (uncond + scale * (cond - uncond))).astype(jnp.bfloat16)


def solution(mesh):
    in_specs = (
        P(None, "cfg", ("clip", "seq"), None),
        P(None, "cfg", None, ("clip", "seq"), None),
        P("cfg", None, ("clip", "seq"), None),
        P(),
        P(),
    )
    out_specs = P(None, ("clip", "seq"), "cfg")
    return jax.shard_map(shards, mesh=mesh, in_specs=in_specs, out_specs=out_specs, check_vma=False)
```

profile of v0, /device:TPU:192, one launch (start us, length us, event | category | flops | bytes accessed | tf_op | source)
XLA Modules:
  0.0 332.4 jit_solution(10178070790870367528)
XLA Ops:
  6.5 0.0 copy-start.2
  6.5 0.0 all-gather.7.cloned.1.call-start
  6.5 1.0 fusion.23
  7.6 0.8 copy.24
  8.4 0.0 all-gather.7.cloned.1.call-update
  8.4 0.0 all-gather.5.cloned.1.call-start
  8.5 1.8 copy.17
  10.2 0.0 all-gather.5.cloned.1.call-update
  10.3 0.6 copy.35
  10.8 0.6 copy.36
  11.4 0.9 fusion.24
  12.4 0.1 reshape_squeeze.23
  12.4 0.1 reshape_squeeze.20
  12.5 0.0 copy-done.2
  12.6 125.4 %all-gather.7.cloned.1.call-done = bf16[1,1,2,1024,2560]{4,2,1,0,3:T(2,128)(2,1)} async-done(((bf16[1,1,2,16,2560]{4,2,1,0,3:T(2,128)(2,1)}), bf16[1,1,2,1024,2560]{4,2,1,0,3:T(2,128)(2,1)}) %all-gather.7.cloned.1.call-update) | async-done | bytes 10485776 | tf_op jit(solution)/shard_map/all_gather | solution.py:53
  138.0 26.1 %copy.25 = bf16[1,1,2,1024,2560]{3,4,2,1,0:T(8,128)(2,1)} copy(bf16[1,1,2,1024,2560]{4,2,1,0,3:T(2,128)(2,1)} %all-gather.7.cloned.1.call-done) | data formatting | bytes 20971520 | tf_op jit(solution)/shard_map/all_gather | solution.py:53
  164.1 14.5 %dynamic_update_slice.7 = bf16[2,1024,2560]{1,2,0:T(8,128)(2,1)} dynamic-update-slice(bf16[2,1024,2560]{1,2,0:T(8,128)(2,1)} %bitcast.34, bf16[2,16,2560]{1,2,0:T(8,128)(2,1)S(1)} %bitcast.40, s32[]{:T(128)} %constant.14.clone.1, s32[]{:T(128)S(6)} %select_n.23, s32[]{:T(128)} %constant.14.clone.1) | dynamic-update-slice | bytes 327684 | tf_op jit(solution)/shard_map/dynamic_update_slice | solution.py:38
  178.6 9.3 %fusion.21 = (bf16[1,1024,2560]{1,2,0:T(8,128)(2,1)}, bf16[1,1024,2560]{1,2,0:T(8,128)(2,1)}) fusion(bf16[2,1024,2560]{1,2,0:T(8,128)(2,1)} %dynamic_update_slice.7), kind=kLoop, calls=%fused_computation.32 | loop fusion | bytes 20971520 | tf_op jit(solution)/shard_map/slice | solution.py:39
  187.9 0.0 copy-start
  187.9 3.6 %fusion.26 = (f32[16,20]{0,1:T(8,128)S(1)}, f32[16,20,1024]{2,0,1:T(8,128)S(1)}) fusion(bf16[1024,20,128]{0,2,1:T(8,128)(2,1)} %bitcast.37, bf16[16,20,128]{2,1,0:T(8,128)(2,1)S(1)} %reshape_squeeze.23), kind=kOutput, calls=%fused_computation.37 | convolution fusion | flops 84541120 | bytes 6636800 | tf_op jit(solution)/shard_map/qhe,khe->qhk/dot_general | solution.py:22
  191.5 0.4 fusion.4
  191.8 0.2 copy-done
  192.1 1.5 fusion.9
  193.6 0.1 stack_reshape.7
  193.7 74.2 %all-gather.5.cloned.1.call-done = bf16[1,2,1024,2560]{3,1,0,2:T(2,128)(2,1)} async-done(((bf16[1,2,16,2560]{3,1,0,2:T(2,128)(2,1)}), bf16[1,2,1024,2560]{3,1,0,2:T(2,128)(2,1)}) %all-gather.5.cloned.1.call-update) | async-done | bytes 10485776 | tf_op jit(solution)/shard_map/all_gather | solution.py:53
  267.9 26.1 %copy.18 = bf16[1,2,1024,2560]{2,3,1,0:T(8,128)(2,1)} copy(bf16[1,2,1024,2560]{3,1,0,2:T(2,128)(2,1)} %all-gather.5.cloned.1.call-done) | data formatting | bytes 20971520 | tf_op jit(solution)/shard_map/all_gather | solution.py:53
  294.0 14.5 %dynamic_update_slice.6 = bf16[2,1024,2560]{1,2,0:T(8,128)(2,1)} dynamic-update-slice(bf16[2,1024,2560]{1,2,0:T(8,128)(2,1)} %bitcast.33, bf16[2,16,2560]{1,2,0:T(8,128)(2,1)S(1)} %bitcast.39, s32[]{:T(128)} %constant.14.clone.1, s32[]{:T(128)S(6)} %select_n.23, s32[]{:T(128)} %constant.14.clone.1) | dynamic-update-slice | bytes 327684 | tf_op jit(solution)/shard_map/dynamic_update_slice | solution.py:38
  308.5 9.3 %fusion.22 = (bf16[1,1024,2560]{1,2,0:T(8,128)(2,1)}, bf16[1,1024,2560]{1,2,0:T(8,128)(2,1)}) fusion(bf16[2,1024,2560]{1,2,0:T(8,128)(2,1)} %dynamic_update_slice.6), kind=kLoop, calls=%fused_computation.33 | loop fusion | bytes 20971520 | tf_op jit(solution)/shard_map/slice | solution.py:39
  317.8 0.0 copy-start.1
  317.8 3.5 %fusion.25 = (f32[16,20]{0,1:T(8,128)S(1)}, f32[16,20,1024]{2,0,1:T(8,128)S(1)}) fusion(bf16[1024,20,128]{0,2,1:T(8,128)(2,1)} %bitcast.38, bf16[16,20,128]{2,1,0:T(8,128)(2,1)S(1)} %reshape_squeeze.20), kind=kOutput, calls=%fused_computation.36 | convolution fusion | flops 84541120 | bytes 6636800 | tf_op jit(solution)/shard_map/qhe,khe->qhk/dot_general | solution.py:22
  321.3 0.4 fusion.2
  321.6 0.2 copy-done.1
  321.8 1.5 fusion.8
  323.3 0.1 stack_reshape.6
  323.5 0.1 collective-permute-start
  323.6 0.2 multiply_add_fusion
  324.5 0.4 collective-permute-done
  324.8 0.7 fusion.18
  (7 shorter events, 0.1 us)
Async XLA Ops:
  6.5 6.0 %copy-start.2 = (s32[2]{0:T(128)S(1)}, s32[2]{0:T(128)}, u32[]{:S(2)}) copy-start(s32[2]{0:T(128)} %param.8) | copy-start | bytes 28
  6.5 131.5 %all-gather.7.cloned.1.call-start = ((), (), s32[]{:S(2)}) async-start(), calls=%async_computation.1 | async-start | bytes 10649600 | tf_op jit(solution)/shard_map/all_gather | solution.py:53
  8.4 259.5 %all-gather.5.cloned.1.call-start = ((), (), s32[]{:S(2)}) async-start(), calls=%async_computation | async-start | bytes 10649600 | tf_op jit(solution)/shard_map/all_gather | solution.py:53
  187.9 4.2 %copy-start = (bf16[1,1024,2560]{1,2,0:T(8,128)(2,1)S(1)}, bf16[1,1024,2560]{1,2,0:T(8,128)(2,1)}, u32[]{:S(2)}) copy-start(bf16[1,1024,2560]{1,2,0:T(8,128)(2,1)} %get-tuple-element.6) | copy-start | bytes 15728644
  317.8 4.0 %copy-start.1 = (bf16[1,1024,2560]{1,2,0:T(8,128)(2,1)S(1)}, bf16[1,1024,2560]{1,2,0:T(8,128)(2,1)}, u32[]{:S(2)}) copy-start(bf16[1,1024,2560]{1,2,0:T(8,128)(2,1)} %get-tuple-element.8) | copy-start | bytes 15728644
  323.5 1.4 collective-permute-start
Sparse Core Ops, SparseCore 0:
  10.7 127.2 all-gather.6
  141.3 126.5 all-gather.4
where the time goes:
time: 339 us; the launch traced here: 332 us
  waiting for transfers between devices  200 us (59%)
  local copies, waits for them, and re-layouts  106 us (31%)
  between operations  14.2 us (4%)
  matrix products  10.1 us (3%)
    all_gather x2, waiting for transfers between devices, shards(): remote_full = lax.all_gather(previous[step_no], 'seq', axis=1, tiled=True)  200 us
    all_gather x2, local copies, waits for them, and re-layouts, shards(): remote_full = lax.all_gather(previous[step_no], 'seq', axis=1, tiled=True)  52.2 us
    dynamic_update_slice x2, local copies, waits for them, and re-layouts, merged_attention(): merged = lax.dynamic_update_slice_in_dim(remote_full, own_kv, first, 1)  29 us
    slice x2, local copies, waits for them, and re-layouts, merged_attention(): return gathered_attention(query_rows, merged[0], merged[1])  18.5 us
    dot_general x2, matrix products, gathered_attention(): jnp.einsum('qhe,khe->qhk', query_heads, key_heads, preferred_element_type...  7.07 us
  transfers between devices with their start and end apart: 3, of which 3 were waited for; matrix products, arithmetic and copies ran while one was open for 18% of the time, Pallas kernels for 0%

commit v1 on v0

v1 whole, which is shorter than its diff:
```python
import functools
import math

import jax
import jax.numpy as jnp
from jax import lax
from jax.experimental import pallas as pl
from jax.experimental.pallas import tpu as pltpu
from jax.sharding import PartitionSpec as P

MESH = pl.DeviceIdType.MESH
HEAD_DIM = 128
HEADS = 20
HALF_HEADS = HEADS // 2
STEPS = 2
UNITS = STEPS * HEADS
TOK = 16
N_SEQ = 64
SEQ_TOKENS = TOK * N_SEQ
CHUNK_SLOTS = 16
CHUNK = CHUNK_SLOTS * TOK
N_CHUNKS = N_SEQ // CHUNK_SLOTS
BRANCH_SHIFT = N_SEQ - UNITS
SCORE_SCALE = 1.0 / math.sqrt(HEAD_DIM)
LOG2E = math.log2(math.e)
MASKED = -1e30


def shifted(place, slot, sign):
    dz, dx, dy = slot % 4, (slot // 4) % 4, slot // 16
    y, z, x = place // 16, (place // 4) % 4, place % 4
    y = (y + sign * dy + 4) % 4
    z = (z + sign * dz + 4) % 4
    x = (x + sign * dx + 4) % 4
    return (y * 4 + z) * 4 + x


def unit_of(place, branch):
    y, z, x = place // 16, (place // 4) % 4, place % 4
    rank = (((y - z + 4) % 4) * 4 + x) * 4 + z
    return rank - BRANCH_SHIFT * branch


def stacked_heads(rows):
    return jnp.concatenate(
        [rows[:, h * HEAD_DIM : (h + 1) * HEAD_DIM] for h in range(HEADS)], axis=0
    )


def with_ones(values):
    return jnp.concatenate([values, jnp.ones_like(values)], axis=1)


def kernel(
    ts_ref, gi_ref, q_hbm, fresh_hbm, stale_hbm, out_ref,
    q_src, kv_src, kv_rx, q_rx, scores_ref, o_buf, lse_buf, o_rx, lse_rx, own_all, own_fin,
    load_sem, kv_sem, q_sem, kv_send, q_send, o_send, lse_send, o_sem, lse_sem, own_send, own_sem,
):
    me = lax.axis_index("seq")
    branch = lax.axis_index("cfg")
    clip = lax.axis_index("clip")
    unit = unit_of(me, branch)
    has_unit = jnp.logical_and(unit >= 0, unit < UNITS)

    barrier = pltpu.get_barrier_semaphore()

    loads = [
        pltpu.make_async_copy(stale_hbm.at[0], kv_src.at[0], load_sem.at[0]),
        pltpu.make_async_copy(fresh_hbm.at[0, 0], kv_src.at[1], load_sem.at[1]),
        pltpu.make_async_copy(q_hbm.at[:, 0], q_src, load_sem.at[2]),
        pltpu.make_async_copy(fresh_hbm.at[1, 0], kv_src.at[2], load_sem.at[3]),
    ]
    for load in loads:
        load.start()

    pl.semaphore_signal(barrier, inc=1, device_id=(me, 1 - branch, clip), device_id_type=MESH)

    @pl.when(has_unit)
    def _():
        def greet(slot, carry):
            pl.semaphore_signal(
                barrier, inc=1, device_id=(shifted(me, slot, 1), branch, clip), device_id_type=MESH
            )
            return carry

        lax.fori_loop(1, N_SEQ, greet, 0)

    for load in loads:
        load.wait()

    @pl.when(has_unit)
    def _():
        pl.semaphore_wait(barrier, UNITS)

    @pl.when(jnp.logical_not(has_unit))
    def _():
        pl.semaphore_wait(barrier, UNITS + 1)

    def kv_block(u):
        return kv_src.at[u // HEADS, :, :, pl.ds(pl.multiple_of(u % HEADS * HEAD_DIM, HEAD_DIM), HEAD_DIM)]

    def q_block(u):
        return q_src.at[u // HEADS, :, pl.ds(pl.multiple_of(u % HEADS * HEAD_DIM, HEAD_DIM), HEAD_DIM)]

    def slot_rows(slot):
        return pl.ds(pl.multiple_of(slot * TOK, TOK), TOK)

    @pl.when(has_unit)
    def _():
        pltpu.make_async_copy(kv_block(unit), kv_rx.at[:, pl.ds(0, TOK), :], kv_sem).start()
        pltpu.make_async_copy(q_block(unit), q_rx.at[pl.ds(0, TOK), :], q_sem.at[0]).start()

    def send_kv(slot, carry):
        there = shifted(me, slot, -1)
        u = unit_of(there, branch)

        @pl.when(jnp.logical_and(u >= 0, u < UNITS))
        def _():
            pltpu.make_async_remote_copy(
                src_ref=kv_block(u),
                dst_ref=kv_rx.at[:, slot_rows(slot), :],
                send_sem=kv_send,
                recv_sem=kv_sem,
                device_id=(there, branch, clip),
                device_id_type=MESH,
            ).start()

        return carry

    lax.fori_loop(1, N_SEQ, send_kv, 0)

    def send_q(slot, carry):
        there = shifted(me, slot, -1)
        u = unit_of(there, branch)

        @pl.when(jnp.logical_and(u >= 0, u < UNITS))
        def _():
            pltpu.make_async_remote_copy(
                src_ref=q_block(u),
                dst_ref=q_rx.at[slot_rows(slot), :],
                send_sem=q_send,
                recv_sem=q_sem.at[slot // CHUNK_SLOTS],
                device_id=(there, branch, clip),
                device_id_type=MESH,
            ).start()

        return carry

    lax.fori_loop(1, N_SEQ, send_q, 0)

    rows = HEADS * TOK
    same_head = (
        lax.broadcasted_iota(jnp.int32, (rows, rows), 0) // TOK
        == lax.broadcasted_iota(jnp.int32, (rows, rows), 1) // TOK
    )
    for s in range(STEPS):
        scores = lax.dot_general(
            stacked_heads(q_src[s]),
            stacked_heads(kv_src[s + 1, 0]),
            (((1,), (1,)), ((), ())),
            preferred_element_type=jnp.float32,
        )
        scores = jnp.where(same_head, scores, MASKED)
        top = jnp.max(scores, axis=1, keepdims=True)
        weights = jnp.exp2((scores - top) * (SCORE_SCALE * LOG2E)).astype(jnp.bfloat16)
        summed = jnp.dot(
            weights, with_ones(stacked_heads(kv_src[s + 1, 1])), preferred_element_type=jnp.float32
        )
        totals = summed[:, HEAD_DIM:]
        own_all[:, s, 0] = (summed[:, :HEAD_DIM] / totals).reshape(2, rows // 2, HEAD_DIM)
        own_all[:, s, 1] = (top * SCORE_SCALE + jnp.log(totals)).reshape(2, rows // 2, HEAD_DIM)

    own_copy = pltpu.make_async_remote_copy(
        src_ref=own_all.at[1 - branch],
        dst_ref=own_fin.at[branch],
        send_sem=own_send,
        recv_sem=own_sem.at[0],
        device_id=(me, 1 - branch, clip),
        device_id_type=MESH,
    )
    own_copy.start()
    own_local = pltpu.make_async_copy(own_all.at[branch], own_fin.at[branch], own_sem.at[1])
    own_local.start()

    channel = (
        branch * (HALF_HEADS * HEAD_DIM)
        + lax.broadcasted_iota(jnp.int32, (HALF_HEADS, 1, HEAD_DIM), 0) * HEAD_DIM
        + lax.broadcasted_iota(jnp.int32, (HALF_HEADS, 1, HEAD_DIM), 2)
    ).astype(jnp.float32)
    frequency = jnp.exp(-math.log(1000.0) * channel / (HEADS * HEAD_DIM))
    gates = [
        1.0 + 0.5 * jnp.sin(ts_ref[s].astype(jnp.float32) * frequency) for s in range(STEPS)
    ]
    scale = 1.0 + 0.5 * gi_ref[0].astype(jnp.float32)

    head = unit % HEADS
    half = head // HALF_HEADS
    unit_step = unit // HEADS

    def send_out(slot, there):
        pltpu.make_async_remote_copy(
            src_ref=o_buf.at[slot_rows(slot), :],
            dst_ref=o_rx.at[branch, unit_step, head % HALF_HEADS],
            send_sem=o_send,
            recv_sem=o_sem,
            device_id=(there, half, clip),
            device_id_type=MESH,
        ).start()
        pltpu.make_async_remote_copy(
            src_ref=lse_buf.at[slot],
            dst_ref=lse_rx.at[branch, unit_step, head % HALF_HEADS],
            send_sem=lse_send,
            recv_sem=lse_sem,
            device_id=(there, half, clip),
            device_id_type=MESH,
        ).start()

    @pl.when(has_unit)
    def _():
        pltpu.make_async_copy(kv_rx, kv_rx, kv_sem).wait()
        same_patch = (
            lax.broadcasted_iota(jnp.int32, (CHUNK, CHUNK), 0) // TOK
            == lax.broadcasted_iota(jnp.int32, (CHUNK, CHUNK), 1) // TOK
        )
        lane_token = lax.broadcasted_iota(jnp.int32, (1, TOK, HEAD_DIM), 2) % TOK
        picked = lane_token == lax.broadcasted_iota(jnp.int32, (1, TOK, HEAD_DIM), 1)
        for c in range(N_CHUNKS):
            here = pl.ds(c * CHUNK, CHUNK)
            pltpu.make_async_copy(q_rx.at[here], q_rx.at[here], q_sem.at[c]).wait()
            scores_ref[...] = lax.dot_general(
                q_rx[here, :], kv_rx[0], (((1,), (1,)), ((), ())), preferred_element_type=jnp.float32
            )
            scores_ref[:, here] = jnp.where(same_patch, MASKED, scores_ref[:, here])
            scores = scores_ref[...]
            top = jnp.max(scores, axis=1, keepdims=True)
            weights = jnp.exp2((scores - top) * (SCORE_SCALE * LOG2E)).astype(jnp.bfloat16)
            summed = jnp.dot(weights, with_ones(kv_rx[1]), preferred_element_type=jnp.float32)
            totals = summed[:, HEAD_DIM:]
            o_buf[here, :] = (summed[:, :HEAD_DIM] / totals).astype(jnp.bfloat16)
            lse = (top * SCORE_SCALE + jnp.log(totals)).reshape(CHUNK_SLOTS, TOK, HEAD_DIM)
            lse_buf[pl.ds(c * CHUNK_SLOTS, CHUNK_SLOTS)] = jnp.sum(
                jnp.where(picked, lse, 0.0), axis=1, keepdims=True
            )
            if c == 0:

                @pl.when(half == branch)
                def _():
                    pltpu.make_async_copy(
                        o_buf.at[pl.ds(0, TOK), :], o_rx.at[branch, unit_step, head % HALF_HEADS], o_sem
                    ).start()
                    pltpu.make_async_copy(
                        lse_buf.at[0], lse_rx.at[branch, unit_step, head % HALF_HEADS], lse_sem
                    ).start()

                @pl.when(half != branch)
                def _():
                    send_out(0, me)

            def send_slot(slot, carry):
                send_out(slot, shifted(me, slot, 1))
                return carry

            lax.fori_loop(max(1, c * CHUNK_SLOTS), (c + 1) * CHUNK_SLOTS, send_slot, 0)

    own_copy.wait_recv()
    own_local.wait()
    pltpu.make_async_copy(lse_rx, lse_rx, lse_sem).wait()
    pltpu.make_async_copy(o_rx, o_rx, o_sem).wait()

    token = lax.broadcasted_iota(jnp.int32, (1, TOK, HEAD_DIM), 1)
    lane = lax.broadcasted_iota(jnp.int32, (1, TOK, HEAD_DIM), 2)

    def attended(b, s):
        remote = o_rx[b, s].astype(jnp.float32)
        remote_lse = jnp.sum(jnp.where(token == lane, lse_rx[b, s], 0.0), axis=2, keepdims=True)
        own = own_fin[b, s, 0].reshape(HALF_HEADS, TOK, HEAD_DIM)
        own_lse = own_fin[b, s, 1].reshape(HALF_HEADS, TOK, HEAD_DIM)
        share = 1.0 / (1.0 + jnp.exp(own_lse - remote_lse))
        return own + share * (remote - own)

    for s in range(STEPS):
        cond = attended(0, s)
        uncond = attended(1, s)
        guided = (gates[s] * (uncond + scale * (cond - uncond))).astype(jnp.bfloat16)
        for h in range(HALF_HEADS):
            out_ref[s, :, h * HEAD_DIM : (h + 1) * HEAD_DIM] = guided[h]

    own_copy.wait_send()

    @pl.when(has_unit)
    def _():
        sent = pl.ds(0, (UNITS - 1) * TOK)
        pltpu.make_async_copy(kv_rx.at[:, sent, :], kv_rx.at[:, sent, :], kv_send).wait()
        pltpu.make_async_copy(q_rx.at[sent], q_rx.at[sent], q_send).wait()

        @pl.when(half == branch)
        def _():
            out_rows, lse_rows = pl.ds(TOK, SEQ_TOKENS - TOK), pl.ds(1, N_SEQ - 1)
            pltpu.make_async_copy(o_buf.at[out_rows], o_buf.at[out_rows], o_send).wait()
            pltpu.make_async_copy(lse_buf.at[lse_rows], lse_buf.at[lse_rows], lse_send).wait()

        @pl.when(half != branch)
        def _():
            pltpu.make_async_copy(o_buf, o_buf, o_send).wait()
            pltpu.make_async_copy(lse_buf, lse_buf, lse_send).wait()

    @pl.when(jnp.logical_not(has_unit))
    def _():
        sent = pl.ds(0, UNITS * TOK)
        pltpu.make_async_copy(kv_rx.at[:, sent, :], kv_rx.at[:, sent, :], kv_send).wait()
        pltpu.make_async_copy(q_rx.at[sent], q_rx.at[sent], q_send).wait()


def shards(queries, fresh_kv, stale_kv, timesteps, guidance_index):
    bf16, f32 = jnp.bfloat16, jnp.float32
    rows = HALF_HEADS * TOK
    dma = pltpu.SemaphoreType.DMA
    return pl.pallas_call(
        kernel,
        out_shape=jax.ShapeDtypeStruct((STEPS, TOK, HALF_HEADS * HEAD_DIM), bf16),
        in_specs=[pl.BlockSpec(memory_space=pltpu.SMEM)] * 2 + [pl.BlockSpec(memory_space=pl.ANY)] * 3,
        out_specs=pl.BlockSpec(memory_space=pltpu.VMEM),
        scratch_shapes=[
            pltpu.VMEM((STEPS, TOK, HEADS * HEAD_DIM), bf16),
            pltpu.VMEM((STEPS + 1, 2, TOK, HEADS * HEAD_DIM), bf16),
            pltpu.VMEM((2, SEQ_TOKENS, HEAD_DIM), bf16),
            pltpu.VMEM((SEQ_TOKENS, HEAD_DIM), bf16),
            pltpu.VMEM((CHUNK, SEQ_TOKENS), f32),
            pltpu.VMEM((SEQ_TOKENS, HEAD_DIM), bf16),
            pltpu.VMEM((N_SEQ, 1, HEAD_DIM), f32),
            pltpu.VMEM((2, STEPS, HALF_HEADS, TOK, HEAD_DIM), bf16),
            pltpu.VMEM((2, STEPS, HALF_HEADS, 1, HEAD_DIM), f32),
            pltpu.VMEM((2, STEPS, 2, rows, HEAD_DIM), f32),
            pltpu.VMEM((2, STEPS, 2, rows, HEAD_DIM), f32),
            dma((4,)), dma, dma((N_CHUNKS,)),
            dma, dma, dma, dma,
            dma, dma, dma, dma((2,)),
        ],
        compiler_params=pltpu.CompilerParams(
            collective_id=0, has_side_effects=True, vmem_limit_bytes=32 * 2**20
        ),
        name="patch_attention",
    )(timesteps, guidance_index, queries, fresh_kv, stale_kv)


def solution(mesh):
    in_specs = (
        P(None, "cfg", ("clip", "seq"), None),
        P(None, "cfg", None, ("clip", "seq"), None),
        P("cfg", None, ("clip", "seq"), None),
        P(),
        P(),
    )
    out_specs = P(None, ("clip", "seq"), "cfg")
    return jax.shard_map(shards, mesh=mesh, in_specs=in_specs, out_specs=out_specs, check_vma=False)
```

time: 339 us -> 45.6 us (0.13)
  the two profiles are of different devices: /device:TPU:192 before, /device:TPU:1 now
where the time goes in v1:
time: 45.6 us; the launch traced here: 45.5 us
  Pallas kernels  41.4 us (91%)
  local copies, waits for them, and re-layouts  3.44 us (8%)
  between operations  0.69 us (2%)
    pallas_call x1, Pallas kernels, shards(): pl.pallas_call(kernel, out_shape=jax.ShapeDtypeStruct((STEPS, TOK, HALF_H...  41.4 us
    unnamed x9, local copies, waits for them, and re-layouts  3.44 us

profile of v1, /device:TPU:1, one launch (start us, length us, event | category | flops | bytes accessed | tf_op | source)
XLA Modules:
  0.0 45.5 jit_solution(15338163670370648686)
XLA Ops:
  0.0 0.0 copy-start.3
  0.7 0.0 copy-done.3
  0.7 0.0 copy-start
  0.7 1.0 %copy-done = bf16[2,1,2,16,2560]{4,3,2,1,0:T(8,128)(2,1)S(1)} copy-done((bf16[2,1,2,16,2560]{4,3,2,1,0:T(8,128)(2,1)S(1)}, bf16[2,1,2,16,2560]{4,3,2,1,0:T(8,128)(2,1)}, u32[]{:S(2)}) %copy-start) | copy-done | bytes 327704
  1.7 0.0 copy-start.1
  1.7 0.9 %copy-done.1 = bf16[2,1,16,2560]{3,2,1,0:T(8,128)(2,1)S(1)} copy-done((bf16[2,1,16,2560]{3,2,1,0:T(8,128)(2,1)S(1)}, bf16[2,1,16,2560]{3,2,1,0:T(8,128)(2,1)}, u32[]{:S(2)}) %copy-start.1) | copy-done | bytes 163864
  2.6 0.0 copy-start.2
  2.6 0.9 %copy-done.2 = bf16[1,2,16,2560]{3,2,1,0:T(8,128)(2,1)S(1)} copy-done((bf16[1,2,16,2560]{3,2,1,0:T(8,128)(2,1)S(1)}, bf16[1,2,16,2560]{3,2,1,0:T(8,128)(2,1)}, u32[]{:S(2)}) %copy-start.2) | copy-done | bytes 163864
  3.5 41.4 %patch_attention.1 = bf16[2,16,1280]{2,1,0:T(8,128)(2,1)S(1)} custom-call(s32[2]{0:T(128)S(1)} %copy-done.3, s32[1]{0:T(128)S(6)} %copy.7.gi_ref, bf16[2,1,16,2560]{3,2,1,0:T(8,128)(2,1)S(1)} %copy-done.1, bf16[2,1,2,16,2560]{4,3,2,1,0:T(8,128)(2,1)S(1)} %copy-done, bf16[1,2,16,2560]{3,2,1,0:T(8,128)(2,1)S(1)} %copy-done.2), custom_call_target="tpu_custom_call" | custom-call | tf_op jit(solution)/shard_map/patch_attention/pallas_call | solution.py:318
  44.8 0.6 %copy.8 = bf16[2,16,1280]{2,1,0:T(8,128)(2,1)} copy(bf16[2,16,1280]{2,1,0:T(8,128)(2,1)S(1)} %patch_attention.1) | data formatting | bytes 163840
Async XLA Ops:
  0.0 0.7 %copy-start.3 = (s32[2]{0:T(128)S(1)}, s32[2]{0:T(128)}, u32[]{:S(2)}) copy-start(s32[2]{0:T(128)} %ts_ref.1) | copy-start | bytes 28
  0.7 1.0 %copy-start = (bf16[2,1,2,16,2560]{4,3,2,1,0:T(8,128)(2,1)S(1)}, bf16[2,1,2,16,2560]{4,3,2,1,0:T(8,128)(2,1)}, u32[]{:S(2)}) copy-start(bf16[2,1,2,16,2560]{4,3,2,1,0:T(8,128)(2,1)} %fresh_hbm.1) | copy-start | bytes 983044
  1.7 0.9 %copy-start.1 = (bf16[2,1,16,2560]{3,2,1,0:T(8,128)(2,1)S(1)}, bf16[2,1,16,2560]{3,2,1,0:T(8,128)(2,1)}, u32[]{:S(2)}) copy-start(bf16[2,1,16,2560]{3,2,1,0:T(8,128)(2,1)} %q_hbm.1) | copy-start | bytes 491524
  2.6 0.9 %copy-start.2 = (bf16[1,2,16,2560]{3,2,1,0:T(8,128)(2,1)S(1)}, bf16[1,2,16,2560]{3,2,1,0:T(8,128)(2,1)}, u32[]{:S(2)}) copy-start(bf16[1,2,16,2560]{3,2,1,0:T(8,128)(2,1)} %stale_hbm.1) | copy-start | bytes 491524

commit v2 on v1

--- a/solution.py
+++ b/solution.py
@@ -26,19 +26,40 @@
 MASKED = -1e30
 
 
-def shifted(place, slot, sign):
-    dz, dx, dy = slot % 4, (slot // 4) % 4, slot // 16
-    y, z, x = place // 16, (place // 4) % 4, place % 4
-    y = (y + sign * dy + 4) % 4
-    z = (z + sign * dz + 4) % 4
-    x = (x + sign * dx + 4) % 4
-    return (y * 4 + z) * 4 + x
-
-
-def unit_of(place, branch):
-    y, z, x = place // 16, (place // 4) % 4, place % 4
-    rank = (((y - z + 4) % 4) * 4 + x) * 4 + z
-    return rank - BRANCH_SHIFT * branch
+PLANES = (2, 1, 3, 0)
+SELF = N_SEQ - 1
+
+
+def rank_of(place):
+    y, z, x = place >> 4, (place >> 2) & 3, place & 3
+    return ((y ^ z) << 4) + (x << 2) + z
+
+
+def holds_unit(unit):
+    return jnp.logical_and(unit >= 0, unit < UNITS)
+
+
+def step_and_head(unit):
+    step = (unit >= HEADS).astype(jnp.int32)
+    return step, unit - step * HEADS
+
+
+def far_to_near(k):
+    return (0x36 >> (2 * k)) & 3
+
+
+def for_slots(chunks, body):
+    def across(i, carry):
+        column = (far_to_near(i >> 2) << 4) + far_to_near(i & 3)
+        for c in chunks:
+            run = functools.partial(body, c, c * CHUNK_SLOTS + i, column + PLANES[c] * 4)
+            if PLANES[c] == 0:
+                pl.when(i < CHUNK_SLOTS - 1)(run)
+            else:
+                run()
+        return carry
+
+    lax.fori_loop(0, CHUNK_SLOTS, across, 0)
 
 
 def stacked_heads(rows):
@@ -52,15 +73,20 @@
 
 
 def kernel(
-    ts_ref, gi_ref, q_hbm, fresh_hbm, stale_hbm, out_ref,
-    q_src, kv_src, kv_rx, q_rx, scores_ref, o_buf, lse_buf, o_rx, lse_rx, own_all, own_fin,
+    ts_hbm, gi_hbm, q_hbm, fresh_hbm, stale_hbm, out_ref,
+    ts_ref, gi_ref, q_src, kv_src, kv_rx, q_rx, scores_ref, o_buf, lse_buf, o_rx, lse_rx, own_all, own_fin,
     load_sem, kv_sem, q_sem, kv_send, q_send, o_send, lse_send, o_sem, lse_sem, own_send, own_sem,
 ):
     me = lax.axis_index("seq")
     branch = lax.axis_index("cfg")
     clip = lax.axis_index("clip")
-    unit = unit_of(me, branch)
-    has_unit = jnp.logical_and(unit >= 0, unit < UNITS)
+    my_rank = rank_of(me)
+    first_rank = BRANCH_SHIFT * branch
+    unit = my_rank - first_rank
+    has_unit = holds_unit(unit)
+    unit_step, head = step_and_head(unit)
+    half = (head >= HALF_HEADS).astype(jnp.int32)
+    half_head = head - half * HALF_HEADS
 
     barrier = pltpu.get_barrier_semaphore()
 
@@ -69,6 +95,8 @@
         pltpu.make_async_copy(fresh_hbm.at[0, 0], kv_src.at[1], load_sem.at[1]),
         pltpu.make_async_copy(q_hbm.at[:, 0], q_src, load_sem.at[2]),
         pltpu.make_async_copy(fresh_hbm.at[1, 0], kv_src.at[2], load_sem.at[3]),
+        pltpu.make_async_copy(ts_hbm, ts_ref, load_sem.at[4]),
+        pltpu.make_async_copy(gi_hbm, gi_ref, load_sem.at[5]),
     ]
     for load in loads:
         load.start()
@@ -77,76 +105,71 @@
 
     @pl.when(has_unit)
     def _():
-        def greet(slot, carry):
+        def greet(chunk, slot, code):
             pl.semaphore_signal(
-                barrier, inc=1, device_id=(shifted(me, slot, 1), branch, clip), device_id_type=MESH
+                barrier, inc=1, device_id=(me ^ code, branch, clip), device_id_type=MESH
             )
-            return carry
-
-        lax.fori_loop(1, N_SEQ, greet, 0)
-
-    for load in loads:
+
+        for_slots((0,), greet)
+        for_slots((1, 2, 3), greet)
+
+    for load in loads[:3]:
         load.wait()
-
-    @pl.when(has_unit)
-    def _():
-        pl.semaphore_wait(barrier, UNITS)
-
-    @pl.when(jnp.logical_not(has_unit))
-    def _():
-        pl.semaphore_wait(barrier, UNITS + 1)
-
-    def kv_block(u):
-        return kv_src.at[u // HEADS, :, :, pl.ds(pl.multiple_of(u % HEADS * HEAD_DIM, HEAD_DIM), HEAD_DIM)]
-
-    def q_block(u):
-        return q_src.at[u // HEADS, :, pl.ds(pl.multiple_of(u % HEADS * HEAD_DIM, HEAD_DIM), HEAD_DIM)]
+    pl.semaphore_wait(barrier, UNITS + 1 - has_unit.astype(jnp.int32))
+
+    def kv_block(step, h):
+        return kv_src.at[step, :, :, pl.ds(pl.multiple_of(h * HEAD_DIM, HEAD_DIM), HEAD_DIM)]
+
+    def q_block(step, h):
+        return q_src.at[step, :, pl.ds(pl.multiple_of(h * HEAD_DIM, HEAD_DIM), HEAD_DIM)]
 
     def slot_rows(slot):
         return pl.ds(pl.multiple_of(slot * TOK, TOK), TOK)
 
-    @pl.when(has_unit)
-    def _():
-        pltpu.make_async_copy(kv_block(unit), kv_rx.at[:, pl.ds(0, TOK), :], kv_sem).start()
-        pltpu.make_async_copy(q_block(unit), q_rx.at[pl.ds(0, TOK), :], q_sem.at[0]).start()
-
-    def send_kv(slot, carry):
-        there = shifted(me, slot, -1)
-        u = unit_of(there, branch)
-
-        @pl.when(jnp.logical_and(u >= 0, u < UNITS))
+    def send_kv(chunk, slot, code):
+        u = (my_rank ^ rank_of(code)) - first_rank
+
+        @pl.when(holds_unit(u))
         def _():
             pltpu.make_async_remote_copy(
-                src_ref=kv_block(u),
+                src_ref=kv_block(*step_and_head(u)),
                 dst_ref=kv_rx.at[:, slot_rows(slot), :],
                 send_sem=kv_send,
                 recv_sem=kv_sem,
-                device_id=(there, branch, clip),
+                device_id=(me ^ code, branch, clip),
                 device_id_type=MESH,
             ).start()
 
-        return carry
-
-    lax.fori_loop(1, N_SEQ, send_kv, 0)
-
-    def send_q(slot, carry):
-        there = shifted(me, slot, -1)
-        u = unit_of(there, branch)
-
-        @pl.when(jnp.logical_and(u >= 0, u < UNITS))
+    def send_q(chunk, slot, code):
+        u = (my_rank ^ rank_of(code)) - first_rank
+
+        @pl.when(holds_unit(u))
         def _():
             pltpu.make_async_remote_copy(
-                src_ref=q_block(u),
+                src_ref=q_block(*step_and_head(u)),
                 dst_ref=q_rx.at[slot_rows(slot), :],
                 send_sem=q_send,
-                recv_sem=q_sem.at[slot // CHUNK_SLOTS],
-                device_id=(there, branch, clip),
+                recv_sem=q_sem.at[chunk],
+                device_id=(me ^ code, branch, clip),
                 device_id_type=MESH,
             ).start()
 
-        return carry
-
-    lax.fori_loop(1, N_SEQ, send_q, 0)
+    for_slots((0,), send_q)
+    for_slots((0,), send_kv)
+    for_slots((1, 2, 3), send_kv)
+    for_slots((1, 2, 3), send_q)
+
+    @pl.when(has_unit)
+    def _():
+        pltpu.make_async_copy(
+            kv_block(unit_step, head), kv_rx.at[:, pl.ds(SELF * TOK, TOK), :], kv_sem
+        ).start()
+        pltpu.make_async_copy(
+            q_block(unit_step, head), q_rx.at[pl.ds(SELF * TOK, TOK), :], q_sem.at[N_CHUNKS - 1]
+        ).start()
+
+    for load in loads[3:]:
+        load.wait()
 
     rows = HEADS * TOK
     same_head = (
@@ -193,25 +216,21 @@
     ]
     scale = 1.0 + 0.5 * gi_ref[0].astype(jnp.float32)
 
-    head = unit % HEADS
-    half = head // HALF_HEADS
-    unit_step = unit // HEADS
-
-    def send_out(slot, there):
+    def send_out(chunk, slot, code):
         pltpu.make_async_remote_copy(
             src_ref=o_buf.at[slot_rows(slot), :],
-            dst_ref=o_rx.at[branch, unit_step, head % HALF_HEADS],
+            dst_ref=o_rx.at[branch, unit_step, half_head],
             send_sem=o_send,
             recv_sem=o_sem,
-            device_id=(there, half, clip),
+            device_id=(me ^ code, half, clip),
             device_id_type=MESH,
         ).start()
         pltpu.make_async_remote_copy(
             src_ref=lse_buf.at[slot],
-            dst_ref=lse_rx.at[branch, unit_step, head % HALF_HEADS],
+            dst_ref=lse_rx.at[branch, unit_step, half_head],
             send_sem=lse_send,
             recv_sem=lse_sem,
-            device_id=(there, half, clip),
+            device_id=(me ^ code, half, clip),
             device_id_type=MESH,
         ).start()
 
@@ -241,26 +260,20 @@
             lse_buf[pl.ds(c * CHUNK_SLOTS, CHUNK_SLOTS)] = jnp.sum(
                 jnp.where(picked, lse, 0.0), axis=1, keepdims=True
             )
-            if c == 0:
-
-                @pl.when(half == branch)
-                def _():
-                    pltpu.make_async_copy(
-                        o_buf.at[pl.ds(0, TOK), :], o_rx.at[branch, unit_step, head % HALF_HEADS], o_sem
-                    ).start()
-                    pltpu.make_async_copy(
-                        lse_buf.at[0], lse_rx.at[branch, unit_step, head % HALF_HEADS], lse_sem
-                    ).start()
-
-                @pl.when(half != branch)
-                def _():
-                    send_out(0, me)
-
-            def send_slot(slot, carry):
-                send_out(slot, shifted(me, slot, 1))
-                return carry
-
-            lax.fori_loop(max(1, c * CHUNK_SLOTS), (c + 1) * CHUNK_SLOTS, send_slot, 0)
+            for_slots((c,), send_out)
+
+        @pl.when(half == branch)
+        def _():
+            pltpu.make_async_copy(
+                o_buf.at[pl.ds(SELF * TOK, TOK), :], o_rx.at[branch, unit_step, half_head], o_sem
+            ).start()
+            pltpu.make_async_copy(
+                lse_buf.at[SELF], lse_rx.at[branch, unit_step, half_head], lse_sem
+            ).start()
+
+        @pl.when(half != branch)
+        def _():
+            send_out(N_CHUNKS - 1, SELF, 0)
 
     own_copy.wait_recv()
     own_local.wait()
@@ -295,7 +308,7 @@
 
         @pl.when(half == branch)
         def _():
-            out_rows, lse_rows = pl.ds(TOK, SEQ_TOKENS - TOK), pl.ds(1, N_SEQ - 1)
+            out_rows, lse_rows = pl.ds(0, SEQ_TOKENS - TOK), pl.ds(0, N_SEQ - 1)
             pltpu.make_async_copy(o_buf.at[out_rows], o_buf.at[out_rows], o_send).wait()
             pltpu.make_async_copy(lse_buf.at[lse_rows], lse_buf.at[lse_rows], lse_send).wait()
 
@@ -318,9 +331,11 @@
     return pl.pallas_call(
         kernel,
         out_shape=jax.ShapeDtypeStruct((STEPS, TOK, HALF_HEADS * HEAD_DIM), bf16),
-        in_specs=[pl.BlockSpec(memory_space=pltpu.SMEM)] * 2 + [pl.BlockSpec(memory_space=pl.ANY)] * 3,
+        in_specs=[pl.BlockSpec(memory_space=pltpu.HBM)] * 5,
         out_specs=pl.BlockSpec(memory_space=pltpu.VMEM),
         scratch_shapes=[
+            pltpu.SMEM((STEPS,), jnp.int32),
+            pltpu.SMEM((1,), jnp.int32),
             pltpu.VMEM((STEPS, TOK, HEADS * HEAD_DIM), bf16),
             pltpu.VMEM((STEPS + 1, 2, TOK, HEADS * HEAD_DIM), bf16),
             pltpu.VMEM((2, SEQ_TOKENS, HEAD_DIM), bf16),
@@ -332,12 +347,12 @@
             pltpu.VMEM((2, STEPS, HALF_HEADS, 1, HEAD_DIM), f32),
             pltpu.VMEM((2, STEPS, 2, rows, HEAD_DIM), f32),
             pltpu.VMEM((2, STEPS, 2, rows, HEAD_DIM), f32),
-            dma((4,)), dma, dma((N_CHUNKS,)),
+            dma((6,)), dma, dma((N_CHUNKS,)),
             dma, dma, dma, dma,
             dma, dma, dma, dma((2,)),
         ],
         compiler_params=pltpu.CompilerParams(
-            collective_id=0, has_side_effects=True, vmem_limit_bytes=32 * 2**20
+            collective_id=0, has_side_effects=True, vmem_limit_bytes=60 * 2**20
         ),
         name="patch_attention",
     )(timesteps, guidance_index, queries, fresh_kv, stale_kv)

time: 45.6 us -> 40.5 us (0.89)
  Pallas kernels: 41.4 us -> 38.1 us
  local copies, waits for them, and re-layouts: 3.44 us -> 1.53 us
    pallas_call x1, Pallas kernels: 41.4 us -> 38.1 us  [shards(): pl.pallas_call(kernel, out_shape=jax.ShapeDtypeStruct((STEPS, TOK, HALF_H...]
    unnamed x9 -> x1, local copies, waits for them, and re-layouts: 3.44 us -> 1.53 us
where the time goes in v2:
time: 40.5 us; the launch traced here: 40.3 us
  Pallas kernels  38.1 us (94%)
  local copies, waits for them, and re-layouts  1.53 us (4%)
  between operations  0.66 us (2%)
    pallas_call x1, Pallas kernels, shards(): pl.pallas_call(kernel, out_shape=jax.ShapeDtypeStruct((STEPS, TOK, HALF_H...  38.1 us
    unnamed x1, local copies, waits for them, and re-layouts  1.53 us

profile of v2, /device:TPU:1, one launch (start us, length us, event | category | flops | bytes accessed | tf_op | source)
XLA Modules:
  0.0 40.3 jit_solution(15077982684947146025)
XLA Ops:
  0.7 38.1 %patch_attention.1 = bf16[2,16,1280]{2,1,0:T(8,128)(2,1)} custom-call(s32[2]{0:T(128)} %ts_hbm.1, s32[1]{0:T(128)S(6)} %copy.7.gi_hbm, bf16[2,1,16,2560]{3,2,1,0:T(8,128)(2,1)} %q_hbm.1, bf16[2,1,2,16,2560]{4,3,2,1,0:T(8,128)(2,1)} %fresh_hbm.1, bf16[1,2,16,2560]{3,2,1,0:T(8,128)(2,1)} %stale_hbm.1), custom_call_target="tpu_custom_call" | custom-call | tf_op jit(solution)/shard_map/patch_attention/pallas_call | solution.py:331
  38.8 1.5 %copy.8 = bf16[2,16,1280]{2,1,0:T(8,128)(2,1)} copy(bf16[2,16,1280]{2,1,0:T(8,128)(2,1)} %patch_attention.1) | data formatting | bytes 163840

commit v3 on v2

--- a/solution.py
+++ b/solution.py
@@ -17,17 +17,17 @@
 TOK = 16
 N_SEQ = 64
 SEQ_TOKENS = TOK * N_SEQ
-CHUNK_SLOTS = 16
-CHUNK = CHUNK_SLOTS * TOK
-N_CHUNKS = N_SEQ // CHUNK_SLOTS
 BRANCH_SHIFT = N_SEQ - UNITS
 SCORE_SCALE = 1.0 / math.sqrt(HEAD_DIM)
 LOG2E = math.log2(math.e)
 MASKED = -1e30
 
 
-PLANES = (2, 1, 3, 0)
-SELF = N_SEQ - 1
+PLANES = 4
+COLUMNS = 16
+FAR_PLANE = 2
+NEAR_PLANES = (1, 3, 0)
+CHUNK = COLUMNS * TOK
 
 
 def rank_of(place):
@@ -48,18 +48,21 @@
     return (0x36 >> (2 * k)) & 3
 
 
-def for_slots(chunks, body):
+def column_code(i):
+    return (far_to_near(i >> 2) << 4) + far_to_near(i & 3)
+
+
+def for_places(planes, body):
     def across(i, carry):
-        column = (far_to_near(i >> 2) << 4) + far_to_near(i & 3)
-        for c in chunks:
-            run = functools.partial(body, c, c * CHUNK_SLOTS + i, column + PLANES[c] * 4)
-            if PLANES[c] == 0:
-                pl.when(i < CHUNK_SLOTS - 1)(run)
+        for plane in planes:
+            run = functools.partial(body, i, column_code(i) + plane * 4)
+            if plane == 0:
+                pl.when(i < COLUMNS - 1)(run)
             else:
                 run()
         return carry
 
-    lax.fori_loop(0, CHUNK_SLOTS, across, 0)
+    lax.fori_loop(0, COLUMNS, across, 0)
 
 
 def stacked_heads(rows):
@@ -74,12 +77,14 @@
 
 def kernel(
     ts_hbm, gi_hbm, q_hbm, fresh_hbm, stale_hbm, out_ref,
-    ts_ref, gi_ref, q_src, kv_src, kv_rx, q_rx, scores_ref, o_buf, lse_buf, o_rx, lse_rx, own_all, own_fin,
+    ts_ref, gi_ref, q_src, kv_src, pack, rx, scores_ref, o_buf, lse_buf, o_rx, lse_rx, own_all, own_fin,
     load_sem, kv_sem, q_sem, kv_send, q_send, o_send, lse_send, o_sem, lse_sem, own_send, own_sem,
 ):
     me = lax.axis_index("seq")
     branch = lax.axis_index("cfg")
     clip = lax.axis_index("clip")
+    my_plane = (me >> 2) & 3
+    my_slot = my_plane * COLUMNS + COLUMNS - 1
     my_rank = rank_of(me)
     first_rank = BRANCH_SHIFT * branch
     unit = my_rank - first_rank
@@ -105,68 +110,73 @@
 
     @pl.when(has_unit)
     def _():
-        def greet(chunk, slot, code):
+        def greet(i, code):
             pl.semaphore_signal(
                 barrier, inc=1, device_id=(me ^ code, branch, clip), device_id_type=MESH
             )
 
-        for_slots((0,), greet)
-        for_slots((1, 2, 3), greet)
+        for_places((FAR_PLANE,), greet)
+        for_places(NEAR_PLANES, greet)
 
     for load in loads[:3]:
         load.wait()
+    for step in range(STEPS):
+        for h in range(HEADS):
+            lanes = pl.ds(h * HEAD_DIM, HEAD_DIM)
+            pack[step * HEADS + h, 0] = q_src[step, :, lanes]
+            pack[step * HEADS + h, 1] = kv_src[step, 0, :, lanes]
+            pack[step * HEADS + h, 2] = kv_src[step, 1, :, lanes]
+
     pl.semaphore_wait(barrier, UNITS + 1 - has_unit.astype(jnp.int32))
-
-    def kv_block(step, h):
-        return kv_src.at[step, :, :, pl.ds(pl.multiple_of(h * HEAD_DIM, HEAD_DIM), HEAD_DIM)]
-
-    def q_block(step, h):
-        return q_src.at[step, :, pl.ds(pl.multiple_of(h * HEAD_DIM, HEAD_DIM), HEAD_DIM)]
 
     def slot_rows(slot):
         return pl.ds(pl.multiple_of(slot * TOK, TOK), TOK)
 
-    def send_kv(chunk, slot, code):
+    def send_kv(i, code):
         u = (my_rank ^ rank_of(code)) - first_rank
 
         @pl.when(holds_unit(u))
         def _():
             pltpu.make_async_remote_copy(
-                src_ref=kv_block(*step_and_head(u)),
-                dst_ref=kv_rx.at[:, slot_rows(slot), :],
+                src_ref=pack.at[u, pl.ds(1, 2)],
+                dst_ref=rx.at[my_plane * COLUMNS + i, pl.ds(1, 2)],
                 send_sem=kv_send,
                 recv_sem=kv_sem,
                 device_id=(me ^ code, branch, clip),
                 device_id_type=MESH,
             ).start()
 
-    def send_q(chunk, slot, code):
+    def send_q(i, code):
         u = (my_rank ^ rank_of(code)) - first_rank
 
         @pl.when(holds_unit(u))
         def _():
             pltpu.make_async_remote_copy(
-                src_ref=q_block(*step_and_head(u)),
-                dst_ref=q_rx.at[slot_rows(slot), :],
+                src_ref=pack.at[u, 0],
+                dst_ref=rx.at[my_plane * COLUMNS + i, 0],
                 send_sem=q_send,
-                recv_sem=q_sem.at[chunk],
+                recv_sem=q_sem.at[my_plane],
                 device_id=(me ^ code, branch, clip),
                 device_id_type=MESH,
             ).start()
 
-    for_slots((0,), send_q)
-    for_slots((0,), send_kv)
-    for_slots((1, 2, 3), send_kv)
-    for_slots((1, 2, 3), send_q)
+    @pl.when(my_plane == 0)
+    def _():
+        for_places((FAR_PLANE,), send_q)
+        for_places(NEAR_PLANES, send_q)
+
+    for_places((FAR_PLANE,), send_kv)
+    for_places(NEAR_PLANES, send_kv)
+
+    @pl.when(my_plane != 0)
+    def _():
+        for_places((FAR_PLANE,), send_q)
+        for_places(NEAR_PLANES, send_q)
 
     @pl.when(has_unit)
     def _():
-        pltpu.make_async_copy(
-            kv_block(unit_step, head), kv_rx.at[:, pl.ds(SELF * TOK, TOK), :], kv_sem
-        ).start()
-        pltpu.make_async_copy(
-            q_block(unit_step, head), q_rx.at[pl.ds(SELF * TOK, TOK), :], q_sem.at[N_CHUNKS - 1]
-        ).start()
+        pltpu.make_async_copy(pack.at[unit, pl.ds(1, 2)], rx.at[my_slot, pl.ds(1, 2)], kv_sem).start()
+        pltpu.make_async_copy(pack.at[unit, 0], rx.at[my_slot, 0], q_sem.at[my_plane]).start()
 
     for load in loads[3:]:
         load.wait()
@@ -178,7 +188,7 @@
     )
     for s in range(STEPS):
         scores = lax.dot_general(
-            stacked_heads(q_src[s]),
+            pack[pl.ds(s * HEADS, HEADS), 0].reshape(rows, HEAD_DIM),
             stacked_heads(kv_src[s + 1, 0]),
             (((1,), (1,)), ((), ())),
             preferred_element_type=jnp.float32,
@@ -216,7 +226,7 @@
     ]
     scale = 1.0 + 0.5 * gi_ref[0].astype(jnp.float32)
 
-    def send_out(chunk, slot, code):
+    def send_out(slot, code):
         pltpu.make_async_remote_copy(
             src_ref=o_buf.at[slot_rows(slot), :],
             dst_ref=o_rx.at[branch, unit_step, half_head],
@@ -234,46 +244,63 @@
             device_id_type=MESH,
         ).start()
 
+    def for_chunk(c):
+        away = my_plane ^ c
+
+        def send_slot(i, carry):
+            @pl.when(jnp.logical_or(away != 0, i < COLUMNS - 1))
+            def _():
+                send_out(c * COLUMNS + i, column_code(i) + away * 4)
+
+            return carry
+
+        lax.fori_loop(0, COLUMNS, send_slot, 0)
+
     @pl.when(has_unit)
     def _():
-        pltpu.make_async_copy(kv_rx, kv_rx, kv_sem).wait()
+        kv_all = rx.at[:, pl.ds(1, 2)]
+        pltpu.make_async_copy(kv_all, kv_all, kv_sem).wait()
+        lane_token = lax.broadcasted_iota(jnp.int32, (1, TOK, HEAD_DIM), 2) % TOK
+        picked = lane_token == lax.broadcasted_iota(jnp.int32, (1, TOK, HEAD_DIM), 1)
         same_patch = (
             lax.broadcasted_iota(jnp.int32, (CHUNK, CHUNK), 0) // TOK
             == lax.broadcasted_iota(jnp.int32, (CHUNK, CHUNK), 1) // TOK
         )
-        lane_token = lax.broadcasted_iota(jnp.int32, (1, TOK, HEAD_DIM), 2) % TOK
-        picked = lane_token == lax.broadcasted_iota(jnp.int32, (1, TOK, HEAD_DIM), 1)
-        for c in range(N_CHUNKS):
-            here = pl.ds(c * CHUNK, CHUNK)
-            pltpu.make_async_copy(q_rx.at[here], q_rx.at[here], q_sem.at[c]).wait()
+        for c in range(PLANES):
+            slots, here = pl.ds(c * COLUMNS, COLUMNS), pl.ds(c * CHUNK, CHUNK)
+            q_chunk = rx.at[slots, 0]
+            pltpu.make_async_copy(q_chunk, q_chunk, q_sem.at[c]).wait()
             scores_ref[...] = lax.dot_general(
-                q_rx[here, :], kv_rx[0], (((1,), (1,)), ((), ())), preferred_element_type=jnp.float32
+                q_chunk[...].reshape(CHUNK, HEAD_DIM),
+                rx[:, 1].reshape(SEQ_TOKENS, HEAD_DIM),
+                (((1,), (1,)), ((), ())),
+                preferred_element_type=jnp.float32,
             )
             scores_ref[:, here] = jnp.where(same_patch, MASKED, scores_ref[:, here])
             scores = scores_ref[...]
             top = jnp.max(scores, axis=1, keepdims=True)
             weights = jnp.exp2((scores - top) * (SCORE_SCALE * LOG2E)).astype(jnp.bfloat16)
-            summed = jnp.dot(weights, with_ones(kv_rx[1]), preferred_element_type=jnp.float32)
+            summed = jnp.dot(weights, with_ones(rx[:, 2].reshape(SEQ_TOKENS, HEAD_DIM)), preferred_element_type=jnp.float32)
             totals = summed[:, HEAD_DIM:]
             o_buf[here, :] = (summed[:, :HEAD_DIM] / totals).astype(jnp.bfloat16)
-            lse = (top * SCORE_SCALE + jnp.log(totals)).reshape(CHUNK_SLOTS, TOK, HEAD_DIM)
-            lse_buf[pl.ds(c * CHUNK_SLOTS, CHUNK_SLOTS)] = jnp.sum(
+            lse = (top * SCORE_SCALE + jnp.log(totals)).reshape(COLUMNS, TOK, HEAD_DIM)
+            lse_buf[slots] = jnp.sum(
                 jnp.where(picked, lse, 0.0), axis=1, keepdims=True
             )
-            for_slots((c,), send_out)
+            for_chunk(c)
 
         @pl.when(half == branch)
         def _():
             pltpu.make_async_copy(
-                o_buf.at[pl.ds(SELF * TOK, TOK), :], o_rx.at[branch, unit_step, half_head], o_sem
+                o_buf.at[slot_rows(my_slot), :], o_rx.at[branch, unit_step, half_head], o_sem
             ).start()
             pltpu.make_async_copy(
-                lse_buf.at[SELF], lse_rx.at[branch, unit_step, half_head], lse_sem
+                lse_buf.at[my_slot], lse_rx.at[branch, unit_step, half_head], lse_sem
             ).start()
 
         @pl.when(half != branch)
         def _():
-            send_out(N_CHUNKS - 1, SELF, 0)
+            send_out(my_slot, 0)
 
     own_copy.wait_recv()
     own_local.wait()
@@ -298,13 +325,16 @@
         for h in range(HALF_HEADS):
             out_ref[s, :, h * HEAD_DIM : (h + 1) * HEAD_DIM] = guided[h]
 
+    def wait_sent(count):
+        kv_sent, q_sent = pack.at[pl.ds(0, count), pl.ds(1, 2)], pack.at[pl.ds(0, count), 0]
+        pltpu.make_async_copy(kv_sent, kv_sent, kv_send).wait()
+        pltpu.make_async_copy(q_sent, q_sent, q_send).wait()
+
     own_copy.wait_send()
 
     @pl.when(has_unit)
     def _():
-        sent = pl.ds(0, (UNITS - 1) * TOK)
-        pltpu.make_async_copy(kv_rx.at[:, sent, :], kv_rx.at[:, sent, :], kv_send).wait()
-        pltpu.make_async_copy(q_rx.at[sent], q_rx.at[sent], q_send).wait()
+        wait_sent(UNITS - 1)
 
         @pl.when(half == branch)
         def _():
@@ -319,9 +349,7 @@
 
     @pl.when(jnp.logical_not(has_unit))
     def _():
-        sent = pl.ds(0, UNITS * TOK)
-        pltpu.make_async_copy(kv_rx.at[:, sent, :], kv_rx.at[:, sent, :], kv_send).wait()
-        pltpu.make_async_copy(q_rx.at[sent], q_rx.at[sent], q_send).wait()
+        wait_sent(UNITS)
 
 
 def shards(queries, fresh_kv, stale_kv, timesteps, guidance_index):
@@ -338,8 +366,8 @@
             pltpu.SMEM((1,), jnp.int32),
             pltpu.VMEM((STEPS, TOK, HEADS * HEAD_DIM), bf16),
             pltpu.VMEM((STEPS + 1, 2, TOK, HEADS * HEAD_DIM), bf16),
-            pltpu.VMEM((2, SEQ_TOKENS, HEAD_DIM), bf16),
-            pltpu.VMEM((SEQ_TOKENS, HEAD_DIM), bf16),
+            pltpu.VMEM((UNITS, 3, TOK, HEAD_DIM), bf16),
+            pltpu.VMEM((N_SEQ, 3, TOK, HEAD_DIM), bf16),
             pltpu.VMEM((CHUNK, SEQ_TOKENS), f32),
             pltpu.VMEM((SEQ_TOKENS, HEAD_DIM), bf16),
             pltpu.VMEM((N_SEQ, 1, HEAD_DIM), f32),
@@ -347,7 +375,7 @@
             pltpu.VMEM((2, STEPS, HALF_HEADS, 1, HEAD_DIM), f32),
             pltpu.VMEM((2, STEPS, 2, rows, HEAD_DIM), f32),
             pltpu.VMEM((2, STEPS, 2, rows, HEAD_DIM), f32),
-            dma((6,)), dma, dma((N_CHUNKS,)),
+            dma((6,)), dma, dma((PLANES,)),
             dma, dma, dma, dma,
             dma, dma, dma, dma((2,)),
         ],

time: 40.5 us -> 38.5 us (0.951)
  Pallas kernels: 38.1 us -> 36.2 us
    pallas_call x1, Pallas kernels: 38.1 us -> 36.2 us  [shards(): pl.pallas_call(kernel, out_shape=jax.ShapeDtypeStruct((STEPS, TOK, HALF_H...]
where the time goes in v3:
time: 38.5 us; the launch traced here: 38.4 us
  Pallas kernels  36.2 us (94%)
  local copies, waits for them, and re-layouts  1.53 us (4%)
  between operations  0.66 us (2%)
    pallas_call x1, Pallas kernels, shards(): pl.pallas_call(kernel, out_shape=jax.ShapeDtypeStruct((STEPS, TOK, HALF_H...  36.2 us
    unnamed x1, local copies, waits for them, and re-layouts  1.53 us

profile of v3, /device:TPU:1, one launch (start us, length us, event | category | flops | bytes accessed | tf_op | source)
XLA Modules:
  0.0 38.4 jit_solution(1373643507588463744)
XLA Ops:
  0.7 36.2 %patch_attention.1 = bf16[2,16,1280]{2,1,0:T(8,128)(2,1)} custom-call(s32[2]{0:T(128)} %ts_hbm.1, s32[1]{0:T(128)S(6)} %copy.7.gi_hbm, bf16[2,1,16,2560]{3,2,1,0:T(8,128)(2,1)} %q_hbm.1, bf16[2,1,2,16,2560]{4,3,2,1,0:T(8,128)(2,1)} %fresh_hbm.1, bf16[1,2,16,2560]{3,2,1,0:T(8,128)(2,1)} %stale_hbm.1), custom_call_target="tpu_custom_call" | custom-call | tf_op jit(solution)/shard_map/patch_attention/pallas_call | solution.py:359
  36.9 1.5 %copy.8 = bf16[2,16,1280]{2,1,0:T(8,128)(2,1)} copy(bf16[2,16,1280]{2,1,0:T(8,128)(2,1)} %patch_attention.1) | data formatting | bytes 163840

commit v4 on v3

--- a/solution.py
+++ b/solution.py
@@ -17,7 +17,9 @@
 TOK = 16
 N_SEQ = 64
 SEQ_TOKENS = TOK * N_SEQ
-BRANCH_SHIFT = N_SEQ - UNITS
+EARLY_UNITS = 12
+LATE_UNITS = UNITS // 2 - EARLY_UNITS
+RELEASE_ORDER = (0xF8635210 - 2**32, 0xFFF7FF94 - 2**32)
 SCORE_SCALE = 1.0 / math.sqrt(HEAD_DIM)
 LOG2E = math.log2(math.e)
 MASKED = -1e30
@@ -30,13 +32,15 @@
 CHUNK = COLUMNS * TOK
 
 
-def rank_of(place):
+def unit_of(place, branch):
     y, z, x = place >> 4, (place >> 2) & 3, place & 3
-    return ((y ^ z) << 4) + (x << 2) + z
-
-
-def holds_unit(unit):
-    return jnp.logical_and(unit >= 0, unit < UNITS)
+    order = jnp.where(y >= 2, RELEASE_ORDER[1], RELEASE_ORDER[0])
+    late_rank = (order >> (((y & 1) << 4) + (x << 2))) & 15
+    early_rank = (((y ^ z) << 2) + x) ^ (15 * branch)
+    late = z >= 2
+    rank = jnp.where(late, late_rank, early_rank)
+    first = jnp.where(late, 2 * EARLY_UNITS + (z - 2) * LATE_UNITS, z * EARLY_UNITS)
+    return first + rank, rank < jnp.where(late, LATE_UNITS, EARLY_UNITS)
 
 
 def step_and_head(unit):
@@ -85,10 +89,7 @@
     clip = lax.axis_index("clip")
     my_plane = (me >> 2) & 3
     my_slot = my_plane * COLUMNS + COLUMNS - 1
-    my_rank = rank_of(me)
-    first_rank = BRANCH_SHIFT * branch
-    unit = my_rank - first_rank
-    has_unit = holds_unit(unit)
+    unit, has_unit = unit_of(me, branch)
     unit_step, head = step_and_head(unit)
     half = (head >= HALF_HEADS).astype(jnp.int32)
     half_head = head - half * HALF_HEADS
@@ -133,9 +134,9 @@
         return pl.ds(pl.multiple_of(slot * TOK, TOK), TOK)
 
     def send_kv(i, code):
-        u = (my_rank ^ rank_of(code)) - first_rank
-
-        @pl.when(holds_unit(u))
+        u, held = unit_of(me ^ code, branch)
+
+        @pl.when(held)
         def _():
             pltpu.make_async_remote_copy(
                 src_ref=pack.at[u, pl.ds(1, 2)],
@@ -147,9 +148,9 @@
             ).start()
 
     def send_q(i, code):
-        u = (my_rank ^ rank_of(code)) - first_rank
-
-        @pl.when(holds_unit(u))
+        u, held = unit_of(me ^ code, branch)
+
+        @pl.when(held)
         def _():
             pltpu.make_async_remote_copy(
                 src_ref=pack.at[u, 0],

time: 38.5 us -> 37 us (0.961)
  the two profiles are of different devices: /device:TPU:1 before, /device:TPU:192 now
where the time goes in v4:
time: 37 us; the launch traced here: 36.9 us
  Pallas kernels  34.7 us (94%)
  local copies, waits for them, and re-layouts  1.53 us (4%)
  between operations  0.66 us (2%)
    pallas_call x1, Pallas kernels, shards(): pl.pallas_call(kernel, out_shape=jax.ShapeDtypeStruct((STEPS, TOK, HALF_H...  34.7 us
    unnamed x1, local copies, waits for them, and re-layouts  1.53 us

profile of v4, /device:TPU:192, one launch (start us, length us, event | category | flops | bytes accessed | tf_op | source)
XLA Modules:
  0.0 36.9 jit_solution(7206483155751545284)
XLA Ops:
  0.7 34.7 %patch_attention.1 = bf16[2,16,1280]{2,1,0:T(8,128)(2,1)} custom-call(s32[2]{0:T(128)} %ts_hbm.1, s32[1]{0:T(128)S(6)} %copy.7.gi_hbm, bf16[2,1,16,2560]{3,2,1,0:T(8,128)(2,1)} %q_hbm.1, bf16[2,1,2,16,2560]{4,3,2,1,0:T(8,128)(2,1)} %fresh_hbm.1, bf16[1,2,16,2560]{3,2,1,0:T(8,128)(2,1)} %stale_hbm.1), custom_call_target="tpu_custom_call" | custom-call | tf_op jit(solution)/shard_map/patch_attention/pallas_call | solution.py:360
  35.4 1.5 %copy.8 = bf16[2,16,1280]{2,1,0:T(8,128)(2,1)} copy(bf16[2,16,1280]{2,1,0:T(8,128)(2,1)} %patch_attention.1) | data formatting | bytes 163840

commit v5 on v4

--- a/solution.py
+++ b/solution.py
@@ -23,6 +23,7 @@
 SCORE_SCALE = 1.0 / math.sqrt(HEAD_DIM)
 LOG2E = math.log2(math.e)
 MASKED = -1e30
+VMEM_GRANT = 538 * 2**20 // 10
 
 
 PLANES = 4
@@ -381,7 +382,7 @@
             dma, dma, dma, dma((2,)),
         ],
         compiler_params=pltpu.CompilerParams(
-            collective_id=0, has_side_effects=True, vmem_limit_bytes=60 * 2**20
+            collective_id=0, has_side_effects=True, vmem_limit_bytes=VMEM_GRANT
         ),
         name="patch_attention",
     )(timesteps, guidance_index, queries, fresh_kv, stale_kv)

time: 37 us -> 35.5 us (0.959)
  local copies, waits for them, and re-layouts: 1.53 us -> 0.64 us
  Pallas kernels: 34.7 us -> 34.1 us
    unnamed x1 -> x3, local copies, waits for them, and re-layouts: 1.53 us -> 0.64 us
    pallas_call x1, Pallas kernels: 34.7 us -> 34.1 us  [shards(): pl.pallas_call(kernel, out_shape=jax.ShapeDtypeStruct((STEPS, TOK, HALF_H...]
where the time goes in v5:
time: 35.5 us; the launch traced here: 35.4 us
  Pallas kernels  34.1 us (96%)
  between operations  0.68 us (2%)
  local copies, waits for them, and re-layouts  0.64 us (2%)
    pallas_call x1, Pallas kernels, shards(): pl.pallas_call(kernel, out_shape=jax.ShapeDtypeStruct((STEPS, TOK, HALF_H...  34.1 us

profile of v5, /device:TPU:192, one launch (start us, length us, event | category | flops | bytes accessed | tf_op | source)
XLA Modules:
  0.0 35.4 jit_solution(2296349653184190601)
XLA Ops:
  0.0 0.0 copy-start
  0.7 0.0 copy-done
  0.7 34.1 %patch_attention.1 = bf16[2,16,1280]{2,1,0:T(8,128)(2,1)S(1)} custom-call(s32[2]{0:T(128)S(1)} %copy-done, s32[1]{0:T(128)S(6)} %copy.7.gi_hbm, bf16[2,1,16,2560]{3,2,1,0:T(8,128)(2,1)} %q_hbm.1, bf16[2,1,2,16,2560]{4,3,2,1,0:T(8,128)(2,1)} %fresh_hbm.1, bf16[1,2,16,2560]{3,2,1,0:T(8,128)(2,1)} %stale_hbm.1), custom_call_target="tpu_custom_call" | custom-call | tf_op jit(solution)/shard_map/patch_attention/pallas_call | solution.py:361
  34.8 0.6 %copy.8 = bf16[2,16,1280]{2,1,0:T(8,128)(2,1)} copy(bf16[2,16,1280]{2,1,0:T(8,128)(2,1)S(1)} %patch_attention.1) | data formatting | bytes 163840
Async XLA Ops:
  0.0 0.7 %copy-start = (s32[2]{0:T(128)S(1)}, s32[2]{0:T(128)}, u32[]{:S(2)}) copy-start(s32[2]{0:T(128)} %ts_hbm.1) | copy-start | bytes 28

commit v6 on v5

--- a/solution.py
+++ b/solution.py
@@ -105,9 +105,6 @@
         pltpu.make_async_copy(ts_hbm, ts_ref, load_sem.at[4]),
         pltpu.make_async_copy(gi_hbm, gi_ref, load_sem.at[5]),
     ]
-    for load in loads:
-        load.start()
-
     pl.semaphore_signal(barrier, inc=1, device_id=(me, 1 - branch, clip), device_id_type=MESH)
 
     @pl.when(has_unit)
@@ -119,6 +116,9 @@
 
         for_places((FAR_PLANE,), greet)
         for_places(NEAR_PLANES, greet)
+
+    for load in loads:
+        load.start()
 
     for load in loads[:3]:
         load.wait()
@@ -249,14 +249,17 @@
     def for_chunk(c):
         away = my_plane ^ c
 
-        def send_slot(i, carry):
-            @pl.when(jnp.logical_or(away != 0, i < COLUMNS - 1))
-            def _():
+        def send_slots(k, carry):
+            for m in range(3):
+                i = 3 * k + m
                 send_out(c * COLUMNS + i, column_code(i) + away * 4)
-
             return carry
 
-        lax.fori_loop(0, COLUMNS, send_slot, 0)
+        lax.fori_loop(0, (COLUMNS - 1) // 3, send_slots, 0)
+
+        @pl.when(away != 0)
+        def _():
+            send_out(c * COLUMNS + COLUMNS - 1, away * 4)
 
     @pl.when(has_unit)
     def _():

time: 35.5 us -> 35.3 us (level)
  no operation moved by 1% of the time
where the time goes in v6:
time: 35.3 us; the launch traced here: 35.2 us
  Pallas kernels  33.9 us (96%)
  between operations  0.68 us (2%)
  local copies, waits for them, and re-layouts  0.64 us (2%)
    pallas_call x1, Pallas kernels, shards(): pl.pallas_call(kernel, out_shape=jax.ShapeDtypeStruct((STEPS, TOK, HALF_H...  33.9 us

profile of v6, /device:TPU:192, one launch (start us, length us, event | category | flops | bytes accessed | tf_op | source)
XLA Modules:
  0.0 35.2 jit_solution(7958400177527850906)
XLA Ops:
  0.0 0.0 copy-start
  0.7 0.0 copy-done
  0.7 33.9 %patch_attention.1 = bf16[2,16,1280]{2,1,0:T(8,128)(2,1)S(1)} custom-call(s32[2]{0:T(128)S(1)} %copy-done, s32[1]{0:T(128)S(6)} %copy.7.gi_hbm, bf16[2,1,16,2560]{3,2,1,0:T(8,128)(2,1)} %q_hbm.1, bf16[2,1,2,16,2560]{4,3,2,1,0:T(8,128)(2,1)} %fresh_hbm.1, bf16[1,2,16,2560]{3,2,1,0:T(8,128)(2,1)} %stale_hbm.1), custom_call_target="tpu_custom_call" | custom-call | tf_op jit(solution)/shard_map/patch_attention/pallas_call | solution.py:364
  34.6 0.6 %copy.8 = bf16[2,16,1280]{2,1,0:T(8,128)(2,1)} copy(bf16[2,16,1280]{2,1,0:T(8,128)(2,1)S(1)} %patch_attention.1) | data formatting | bytes 163840
Async XLA Ops:
  0.0 0.7 %copy-start = (s32[2]{0:T(128)S(1)}, s32[2]{0:T(128)}, u32[]{:S(2)}) copy-start(s32[2]{0:T(128)} %ts_hbm.1) | copy-start | bytes 28

commit v7 on v6

--- a/solution.py
+++ b/solution.py
@@ -233,7 +233,7 @@
             src_ref=o_buf.at[slot_rows(slot), :],
             dst_ref=o_rx.at[branch, unit_step, half_head],
             send_sem=o_send,
-            recv_sem=o_sem,
+            recv_sem=o_sem.at[unit_step],
             device_id=(me ^ code, half, clip),
             device_id_type=MESH,
         ).start()
@@ -241,7 +241,7 @@
             src_ref=lse_buf.at[slot],
             dst_ref=lse_rx.at[branch, unit_step, half_head],
             send_sem=lse_send,
-            recv_sem=lse_sem,
+            recv_sem=lse_sem.at[unit_step],
             device_id=(me ^ code, half, clip),
             device_id_type=MESH,
         ).start()
@@ -297,10 +297,10 @@
         @pl.when(half == branch)
         def _():
             pltpu.make_async_copy(
-                o_buf.at[slot_rows(my_slot), :], o_rx.at[branch, unit_step, half_head], o_sem
+                o_buf.at[slot_rows(my_slot), :], o_rx.at[branch, unit_step, half_head], o_sem.at[unit_step]
             ).start()
             pltpu.make_async_copy(
-                lse_buf.at[my_slot], lse_rx.at[branch, unit_step, half_head], lse_sem
+                lse_buf.at[my_slot], lse_rx.at[branch, unit_step, half_head], lse_sem.at[unit_step]
             ).start()
 
         @pl.when(half != branch)
@@ -309,8 +309,6 @@
 
     own_copy.wait_recv()
     own_local.wait()
-    pltpu.make_async_copy(lse_rx, lse_rx, lse_sem).wait()
-    pltpu.make_async_copy(o_rx, o_rx, o_sem).wait()
 
     token = lax.broadcasted_iota(jnp.int32, (1, TOK, HEAD_DIM), 1)
     lane = lax.broadcasted_iota(jnp.int32, (1, TOK, HEAD_DIM), 2)
@@ -324,6 +322,8 @@
         return own + share * (remote - own)
 
     for s in range(STEPS):
+        pltpu.make_async_copy(lse_rx.at[:, s], lse_rx.at[:, s], lse_sem.at[s]).wait()
+        pltpu.make_async_copy(o_rx.at[:, s], o_rx.at[:, s], o_sem.at[s]).wait()
         cond = attended(0, s)
         uncond = attended(1, s)
         guided = (gates[s] * (uncond + scale * (cond - uncond))).astype(jnp.bfloat16)
@@ -382,7 +382,7 @@
             pltpu.VMEM((2, STEPS, 2, rows, HEAD_DIM), f32),
             dma((6,)), dma, dma((PLANES,)),
             dma, dma, dma, dma,
-            dma, dma, dma, dma((2,)),
+            dma((STEPS,)), dma((STEPS,)), dma, dma((2,)),
         ],
         compiler_params=pltpu.CompilerParams(
             collective_id=0, has_side_effects=True, vmem_limit_bytes=VMEM_GRANT

time: 35.3 us -> 35.5 us (level)
  no operation moved by 1% of the time
where the time goes in v7:
time: 35.5 us; the launch traced here: 35.4 us
  Pallas kernels  34 us (96%)
  between operations  0.68 us (2%)
  local copies, waits for them, and re-layouts  0.64 us (2%)
    pallas_call x1, Pallas kernels, shards(): pl.pallas_call(kernel, out_shape=jax.ShapeDtypeStruct((STEPS, TOK, HALF_H...  34 us

profile of v7, /device:TPU:192, one launch (start us, length us, event | category | flops | bytes accessed | tf_op | source)
XLA Modules:
  0.0 35.4 jit_solution(4640017282740860048)
XLA Ops:
  0.0 0.0 copy-start
  0.7 0.0 copy-done
  0.7 34.0 %patch_attention.1 = bf16[2,16,1280]{2,1,0:T(8,128)(2,1)S(1)} custom-call(s32[2]{0:T(128)S(1)} %copy-done, s32[1]{0:T(128)S(6)} %copy.7.gi_hbm, bf16[2,1,16,2560]{3,2,1,0:T(8,128)(2,1)} %q_hbm.1, bf16[2,1,2,16,2560]{4,3,2,1,0:T(8,128)(2,1)} %fresh_hbm.1, bf16[1,2,16,2560]{3,2,1,0:T(8,128)(2,1)} %stale_hbm.1), custom_call_target="tpu_custom_call" | custom-call | tf_op jit(solution)/shard_map/patch_attention/pallas_call | solution.py:364
  34.7 0.6 %copy.8 = bf16[2,16,1280]{2,1,0:T(8,128)(2,1)} copy(bf16[2,16,1280]{2,1,0:T(8,128)(2,1)S(1)} %patch_attention.1) | data formatting | bytes 163840
Async XLA Ops:
  0.0 0.7 %copy-start = (s32[2]{0:T(128)S(1)}, s32[2]{0:T(128)}, u32[]{:S(2)}) copy-start(s32[2]{0:T(128)} %ts_hbm.1) | copy-start | bytes 28

commit v8 on v6

--- a/solution.py
+++ b/solution.py
@@ -128,57 +128,6 @@
             pack[step * HEADS + h, 0] = q_src[step, :, lanes]
             pack[step * HEADS + h, 1] = kv_src[step, 0, :, lanes]
             pack[step * HEADS + h, 2] = kv_src[step, 1, :, lanes]
-
-    pl.semaphore_wait(barrier, UNITS + 1 - has_unit.astype(jnp.int32))
-
-    def slot_rows(slot):
-        return pl.ds(pl.multiple_of(slot * TOK, TOK), TOK)
-
-    def send_kv(i, code):
-        u, held = unit_of(me ^ code, branch)
-
-        @pl.when(held)
-        def _():
-            pltpu.make_async_remote_copy(
-                src_ref=pack.at[u, pl.ds(1, 2)],
-                dst_ref=rx.at[my_plane * COLUMNS + i, pl.ds(1, 2)],
-                send_sem=kv_send,
-                recv_sem=kv_sem,
-                device_id=(me ^ code, branch, clip),
-                device_id_type=MESH,
-            ).start()
-
-    def send_q(i, code):
-        u, held = unit_of(me ^ code, branch)
-
-        @pl.when(held)
-        def _():
-            pltpu.make_async_remote_copy(
-                src_ref=pack.at[u, 0],
-                dst_ref=rx.at[my_plane * COLUMNS + i, 0],
-                send_sem=q_send,
-                recv_sem=q_sem.at[my_plane],
-                device_id=(me ^ code, branch, clip),
-                device_id_type=MESH,
-            ).start()
-
-    @pl.when(my_plane == 0)
-    def _():
-        for_places((FAR_PLANE,), send_q)
-        for_places(NEAR_PLANES, send_q)
-
-    for_places((FAR_PLANE,), send_kv)
-    for_places(NEAR_PLANES, send_kv)
-
-    @pl.when(my_plane != 0)
-    def _():
-        for_places((FAR_PLANE,), send_q)
-        for_places(NEAR_PLANES, send_q)
-
-    @pl.when(has_unit)
-    def _():
-        pltpu.make_async_copy(pack.at[unit, pl.ds(1, 2)], rx.at[my_slot, pl.ds(1, 2)], kv_sem).start()
-        pltpu.make_async_copy(pack.at[unit, 0], rx.at[my_slot, 0], q_sem.at[my_plane]).start()
 
     for load in loads[3:]:
         load.wait()
@@ -205,6 +154,68 @@
         own_all[:, s, 0] = (summed[:, :HEAD_DIM] / totals).reshape(2, rows // 2, HEAD_DIM)
         own_all[:, s, 1] = (top * SCORE_SCALE + jnp.log(totals)).reshape(2, rows // 2, HEAD_DIM)
 
+    channel = (
+        branch * (HALF_HEADS * HEAD_DIM)
+        + lax.broadcasted_iota(jnp.int32, (HALF_HEADS, 1, HEAD_DIM), 0) * HEAD_DIM
+        + lax.broadcasted_iota(jnp.int32, (HALF_HEADS, 1, HEAD_DIM), 2)
+    ).astype(jnp.float32)
+    frequency = jnp.exp(-math.log(1000.0) * channel / (HEADS * HEAD_DIM))
+    gates = [
+        1.0 + 0.5 * jnp.sin(ts_ref[s].astype(jnp.float32) * frequency) for s in range(STEPS)
+    ]
+    scale = 1.0 + 0.5 * gi_ref[0].astype(jnp.float32)
+
+    pl.semaphore_wait(barrier, UNITS + 1 - has_unit.astype(jnp.int32))
+
+    def slot_rows(slot):
+        return pl.ds(pl.multiple_of(slot * TOK, TOK), TOK)
+
+    def send_kv(i, code):
+        u, held = unit_of(me ^ code, branch)
+
+        @pl.when(held)
+        def _():
+            pltpu.make_async_remote_copy(
+                src_ref=pack.at[u, pl.ds(1, 2)],
+                dst_ref=rx.at[my_plane * COLUMNS + i, pl.ds(1, 2)],
+                send_sem=kv_send,
+                recv_sem=kv_sem,
+                device_id=(me ^ code, branch, clip),
+                device_id_type=MESH,
+            ).start()
+
+    def send_q(i, code):
+        u, held = unit_of(me ^ code, branch)
+
+        @pl.when(held)
+        def _():
+            pltpu.make_async_remote_copy(
+                src_ref=pack.at[u, 0],
+                dst_ref=rx.at[my_plane * COLUMNS + i, 0],
+                send_sem=q_send,
+                recv_sem=q_sem.at[my_plane],
+                device_id=(me ^ code, branch, clip),
+                device_id_type=MESH,
+            ).start()
+
+    @pl.when(my_plane == 0)
+    def _():
+        for_places((FAR_PLANE,), send_q)
+        for_places(NEAR_PLANES, send_q)
+
+    for_places((FAR_PLANE,), send_kv)
+    for_places(NEAR_PLANES, send_kv)
+
+    @pl.when(my_plane != 0)
+    def _():
+        for_places((FAR_PLANE,), send_q)
+        for_places(NEAR_PLANES, send_q)
+
+    @pl.when(has_unit)
+    def _():
+        pltpu.make_async_copy(pack.at[unit, pl.ds(1, 2)], rx.at[my_slot, pl.ds(1, 2)], kv_sem).start()
+        pltpu.make_async_copy(pack.at[unit, 0], rx.at[my_slot, 0], q_sem.at[my_plane]).start()
+
     own_copy = pltpu.make_async_remote_copy(
         src_ref=own_all.at[1 - branch],
         dst_ref=own_fin.at[branch],
@@ -216,17 +227,6 @@
     own_copy.start()
     own_local = pltpu.make_async_copy(own_all.at[branch], own_fin.at[branch], own_sem.at[1])
     own_local.start()
-
-    channel = (
-        branch * (HALF_HEADS * HEAD_DIM)
-        + lax.broadcasted_iota(jnp.int32, (HALF_HEADS, 1, HEAD_DIM), 0) * HEAD_DIM
-        + lax.broadcasted_iota(jnp.int32, (HALF_HEADS, 1, HEAD_DIM), 2)
-    ).astype(jnp.float32)
-    frequency = jnp.exp(-math.log(1000.0) * channel / (HEADS * HEAD_DIM))
-    gates = [
-        1.0 + 0.5 * jnp.sin(ts_ref[s].astype(jnp.float32) * frequency) for s in range(STEPS)
-    ]
-    scale = 1.0 + 0.5 * gi_ref[0].astype(jnp.float32)
 
     def send_out(slot, code):
         pltpu.make_async_remote_copy(

time: 35.3 us -> 35.3 us (level)
  no operation moved by 1% of the time
where the time goes in v8:
time: 35.3 us; the launch traced here: 35.2 us
  Pallas kernels  33.9 us (96%)
  between operations  0.68 us (2%)
  local copies, waits for them, and re-layouts  0.64 us (2%)
    pallas_call x1, Pallas kernels, shards(): pl.pallas_call(kernel, out_shape=jax.ShapeDtypeStruct((STEPS, TOK, HALF_H...  33.9 us

profile of v8, /device:TPU:192, one launch (start us, length us, event | category | flops | bytes accessed | tf_op | source)
XLA Modules:
  0.0 35.2 jit_solution(10873057267880928272)
XLA Ops:
  0.0 0.0 copy-start
  0.7 0.0 copy-done
  0.7 33.9 %patch_attention.1 = bf16[2,16,1280]{2,1,0:T(8,128)(2,1)S(1)} custom-call(s32[2]{0:T(128)S(1)} %copy-done, s32[1]{0:T(128)S(6)} %copy.7.gi_hbm, bf16[2,1,16,2560]{3,2,1,0:T(8,128)(2,1)} %q_hbm.1, bf16[2,1,2,16,2560]{4,3,2,1,0:T(8,128)(2,1)} %fresh_hbm.1, bf16[1,2,16,2560]{3,2,1,0:T(8,128)(2,1)} %stale_hbm.1), custom_call_target="tpu_custom_call" | custom-call | tf_op jit(solution)/shard_map/patch_attention/pallas_call | solution.py:364
  34.6 0.6 %copy.8 = bf16[2,16,1280]{2,1,0:T(8,128)(2,1)} copy(bf16[2,16,1280]{2,1,0:T(8,128)(2,1)S(1)} %patch_attention.1) | data formatting | bytes 163840
Async XLA Ops:
  0.0 0.7 %copy-start = (s32[2]{0:T(128)S(1)}, s32[2]{0:T(128)}, u32[]{:S(2)}) copy-start(s32[2]{0:T(128)} %ts_hbm.1) | copy-start | bytes 28
